TPU v7x, 32 devices: a whole 2x2x4 slice. The times are simulated.
32 devices in a mesh: leaf: 8 (over y, x, core), rep: 4 (over z).
Axes of the slice: x: 2, y: 2, z: 4, core: 2. Of those that a mesh axis runs over, the one named last changes fastest.
Arguments:
- local_right: float32 [8, 4, 2048, 128], P('leaf', 'rep'), may hold values from -6 to 6
- local_inverse: bfloat16 [8, 4, 16, 128, 128], P('leaf', 'rep'), may hold values from -1 to 1.4, as said below
- local_below: bfloat16 [8, 4, 15, 128, 128], P('leaf', 'rep'), may hold values from -0.5 to 0.5
- local_parent: int32 [8, 4, 15], P('leaf', 'rep'), may hold values from 1 to 15, as said below
- local_coupling: bfloat16 [8, 4, 3, 384, 2048], P('leaf', 'rep'), may hold values from -0.1 to 0.1
- separator_right: float32 [7, 384, 128], replicated, may hold values from -6 to 6
- separator_inverse: bfloat16 [7, 3, 128, 128], replicated, may hold values from -1 to 1.4, as said below
- separator_lower: bfloat16 [7, 384, 384], replicated, may hold values from -0.3125 to 0.3125
- parent_coupling: bfloat16 [6, 384, 384], replicated, may hold values from -0.3125 to 0.3125
Outputs:
- local_solution: float32 [8, 4, 2048, 128], P('leaf', 'rep')
- separator_solution: float32 [8, 3, 384, 128], P('leaf')
Inputs may be any that keep to these rules, and one draw needn't show every extreme that they name: `local_parent`: entry k of a device's list is larger than k. `local_inverse`: every block is lower triangular. `separator_inverse`: every block is lower triangular.
All inputs are finite; a program needn't handle non-finite values.
Results may differ from a plain program's by a relative error of at most 0.035.
Values sent between devices are 32-bit elements; how exact they have to be, the bound alone decides.
A program may use at most 128 MiB of HBM per device.

v0:
```python
import jax
import jax.numpy as jnp
from jax import lax
from jax.sharding import PartitionSpec as P

NB = 128
LB = 16
SB = 3


def swapped(value, axis, distance):
    mask = 2**distance
    pairs = [(source, source ^ mask) for source in range(lax.axis_size(axis))]
    return lax.ppermute(value, axis, pairs)


def apply_lower(matrix, vector):
    return jnp.dot(matrix, vector.astype(jnp.bfloat16), preferred_element_type=jnp.float32)


def apply_upper(matrix, vector):
    return jnp.dot(matrix.T, vector.astype(jnp.bfloat16), preferred_element_type=jnp.float32)


def right_lower(vector_rows, matrix):
    return jnp.dot(vector_rows.astype(jnp.bfloat16), matrix.T, preferred_element_type=jnp.float32)


def right_upper(vector_rows, matrix):
    return jnp.dot(vector_rows.astype(jnp.bfloat16), matrix, preferred_element_type=jnp.float32)


def block_lookup_tables(below, parents):
    targets = jnp.concatenate([parents, jnp.full((1,), LB, jnp.int32)])
    padded = jnp.concatenate([below, jnp.zeros((1, NB, NB), below.dtype)], axis=0)
    orders = jnp.arange(LB, dtype=jnp.int32)
    return (targets, padded, orders)


def local_forward(righthand, inverse, below, parents):
    columns = righthand.shape[1]
    blocks = righthand.reshape(LB, NB, columns)
    targets, padded, orders = block_lookup_tables(below, parents)

    def advance(carried, items):
        current, inv_block, low_block, target, number = items
        result = apply_lower(inv_block, current - carried[number])
        carried = carried.at[target].add(apply_lower(low_block, result))
        return (carried, result)

    start = jnp.zeros((LB + 1, NB, columns), jnp.float32)
    _, results = lax.scan(advance, start, (blocks, inverse, padded, targets, orders))
    return results.reshape(LB * NB, columns)


def local_backward(forward, update_terms, inverse, below, parents):
    columns = forward.shape[1]
    remains = (forward - update_terms).reshape(LB, NB, columns)
    targets, padded, orders = block_lookup_tables(below, parents)

    def retreat(carried, items):
        current, inv_block, low_block, target, number = items
        result = apply_upper(inv_block, current - apply_upper(low_block, carried[target]))
        carried = carried.at[number].set(result.astype(jnp.bfloat16))
        return (carried, result)

    start = jnp.zeros((LB + 1, NB, columns), jnp.bfloat16)
    _, results = lax.scan(retreat, start, (remains, inverse, padded, targets, orders), reverse=True)
    return results.reshape(LB * NB, columns)


def separator_forward(righthand, inverse, lowerpart):
    solved = []
    rounded = []
    for position in range(SB):
        current = righthand[:, position * NB : (position + 1) * NB]
        if position > 0:
            earlier = jnp.concatenate(rounded, axis=1)
            current = current - jnp.dot(
                earlier,
                lowerpart[position * NB : (position + 1) * NB, : position * NB].T,
                preferred_element_type=jnp.float32,
            )
        result = right_lower(current, inverse[position])
        solved.append(result)
        rounded.append(result.astype(jnp.bfloat16))
    return (jnp.concatenate(solved, axis=1), jnp.concatenate(rounded, axis=1))


def separator_backward(righthand, inverse, lowerpart):
    solved = [None] * SB
    rounded = [None] * SB
    for position in reversed(range(SB)):
        current = righthand[:, position * NB : (position + 1) * NB]
        if position < SB - 1:
            later = jnp.concatenate(rounded[position + 1 :], axis=1)
            current = current - right_upper(
                later, lowerpart[(position + 1) * NB :, position * NB : (position + 1) * NB]
            )
        result = right_upper(current, inverse[position])
        solved[position] = result
        rounded[position] = result.astype(jnp.bfloat16)
    return (jnp.concatenate(solved, axis=1), jnp.concatenate(rounded, axis=1))


def pick_entry(array, number):
    return lax.dynamic_index_in_dim(array, number, 0, keepdims=False)


def separator_chain(updates, separator_right, separator_inverse, separator_lower, parent_coupling):
    leaf_count = lax.axis_size("leaf")
    levels = leaf_count.bit_length() - 1
    leaf_index = lax.axis_index("leaf")
    remaining = updates
    forward_seps = []
    numbers = []
    inverse_blocks = []
    lowers = []
    for height in range(1, levels + 1):
        remaining = remaining + swapped(remaining, "leaf", height - 1)
        number = (leaf_count >> height) - 1 + (leaf_index >> height)
        right_rows = pick_entry(separator_right, number).T
        inverse = pick_entry(separator_inverse, number)
        lowerpart = pick_entry(separator_lower, number)
        result, result_round = separator_forward(right_rows - remaining[0], inverse, lowerpart)
        forward_seps.append(result)
        numbers.append(number)
        inverse_blocks.append(inverse)
        lowers.append(lowerpart)
        if height < levels:
            coupling_matrix = pick_entry(parent_coupling, number - 1)
            remaining = remaining[1:]
            remaining = remaining.at[0].add(
                jnp.dot(result_round, coupling_matrix.T, preferred_element_type=jnp.float32)
            )
    solutions = [None] * levels
    above_round = None
    for height in range(levels, 0, -1):
        upward = forward_seps[height - 1]
        if height < levels:
            coupling_matrix = pick_entry(parent_coupling, numbers[height - 1] - 1)
            upward = upward - right_upper(above_round, coupling_matrix)
        result, above_round = separator_backward(
            upward, inverse_blocks[height - 1], lowers[height - 1]
        )
        solutions[height - 1] = result
    return jnp.stack(solutions, axis=0)


def on_device(
    local_right,
    local_inverse,
    local_below,
    local_parent,
    local_coupling,
    separator_right,
    separator_inverse,
    separator_lower,
    parent_coupling,
):
    forward = local_forward(
        local_right[0, 0], local_inverse[0, 0], local_below[0, 0], local_parent[0, 0]
    )
    coupling_matrix = local_coupling[0, 0]
    forward_pass_rounded = forward.astype(jnp.bfloat16)
    partials = jnp.einsum(
        "ekx,xn->enk", coupling_matrix, forward_pass_rounded, preferred_element_type=jnp.float32
    )
    updates = lax.psum(partials, "rep")
    solved = separator_chain(
        updates, separator_right, separator_inverse, separator_lower, parent_coupling
    )
    rounded_solution_rows = solved.astype(jnp.bfloat16)
    update_terms = jnp.einsum(
        "apy,anp->yn", coupling_matrix, rounded_solution_rows, preferred_element_type=jnp.float32
    )
    local_solution = local_backward(
        forward, update_terms, local_inverse[0, 0], local_below[0, 0], local_parent[0, 0]
    )
    return (local_solution[None, None], jnp.swapaxes(solved, 1, 2)[None])


def solution(mesh):
    in_specs = (
        P("leaf", "rep", None, None),
        P("leaf", "rep", None, None, None),
        P("leaf", "rep", None, None, None),
        P("leaf", "rep", None),
        P("leaf", "rep", None, None, None),
        P(),
        P(),
        P(),
        P(),
    )
    out_specs = (P("leaf", "rep", None, None), P("leaf", None, None, None))
    return jax.shard_map(
        on_device, mesh=mesh, in_specs=in_specs, out_specs=out_specs, check_vma=False
    )
```

profile of v0, /device:TPU:0, one launch (start us, length us, event | category | flops | bytes accessed | tf_op | source)
XLA Modules:
  0.0 410.2 jit_solution(14303467852418851237)
XLA Ops:
  10.4 145.7 %while.32 = (s32[]{:T(128)}, f32[17,128,128]{2,1,0:T(8,128)}, f32[16,128,128]{2,1,0:T(8,128)S(1)}, s32[16]{0:T(128)S(1)}, bf16[16,128,128]{2,1,0:T(8,128)(2,1)S(...) while((s32[]{:T(128)}, f32[17,128,128]{2,1,0:T(8,128)}, ...), condition=%wide.region_2.3_spmd, body=%wide.region_0.2_spmd.sunk | while | flops 8470553 | bytes 462066 | solution.py:52
  17.3 2.2 fusion.311
  26.4 2.2 fusion.311
  35.5 2.2 fusion.311
  44.6 2.2 fusion.311
  53.7 2.2 fusion.311
  62.8 2.2 fusion.311
  71.9 2.2 fusion.311
  81.0 2.2 fusion.311
  90.1 2.2 fusion.311
  99.2 2.2 fusion.311
  108.3 2.2 fusion.311
  117.4 2.2 fusion.311
  126.5 2.2 fusion.311
  135.6 2.2 fusion.311
  144.7 2.2 fusion.311
  153.8 2.2 fusion.311
  156.2 4.9 %fusion.40 = f32[3,128,384]{2,1,0:T(8,128)} fusion(bf16[2048,128,1]{1,0,2:T(8,128)(2,1)S(1)} %bitcast.264, bf16[1,1,3,384,2048]{4,3,2,1,0:T(8,128)(2,1)} %param.25), kind=kOutput, calls=%fused_computation.38 | convolution fusion | flops 603979776 | bytes 5832704 | tf_op jit(solution)/shard_map/ekx,xn->enk/dot_general | solution.py:166
  161.1 42.0 %all-reduce.3.cloned.1.call-done = f32[3,128,384]{2,1,0:T(8,128)} async-done(((f32[3,128,384]{2,1,0:T(8,128)}), f32[3,128,384]{2,1,0:T(8,128)}) %all-reduce.3.cloned.1.call-update) | async-done | bytes 589840 | tf_op jit(solution)/shard_map/psum | solution.py:169
  205.8 2.1 dynamic-slice_bitcast_fusion
  219.9 8.6 %collective-permute-done.1 = f32[2,128,384]{2,1,0:T(8,128)} collective-permute-done((f32[2,128,384]{2,1,0:T(8,128)}, f32[2,128,384]{2,1,0:T(8,128)}, u32[]{:S(2)}, u32[]{:S(2)}) %collective-permute-start.1) | collective-permute-done | bytes 393248 | tf_op jit(solution)/shard_map/ppermute | solution.py:14
  242.7 2.3 collective-permute-done.2
  264.3 4.2 %fusion.37 = f32[2048,128]{0,1:T(8,128)} fusion(f32[2048,128]{0,1:T(8,128)S(1)} %copy-done.1, bf16[1,1,3,384,2048]{4,3,2,1,0:T(8,128)(2,1)} %param.25, f32[1,128,384]{1,2,0:T(8,128)S(1)} %maximum_bitcast_fusion.2, f32[1,128,384]{1,2,0:T(8,128)S(1)} %get-tuple-element.337, f32[1,128,384]{1,2,0:T(8,128)S(1)} %get-tuple-element.336), kind=kOutput, calls=%fused_computation.37 | convolution fusion | flops 604536832 | bytes 7405568 | tf_op jit(solution)/shard_map/apy,anp->yn/dot_general | solution.py:174
  271.3 132.0 %while.33 = (s32[]{:T(128)}, bf16[17,128,128]{2,1,0:T(8,128)(2,1)S(1)}, f32[16,128,128]{2,1,0:T(8,128)}, s32[16]{0:T(128)S(1)}, bf16[16,128,128]{2,1,0:T(8,128)(...) while((s32[]{:T(128)}, ...), condition=%wide.region_6.7_spmd, body=%wide.region_4.6_spmd.sunk | while | flops 8454170 | bytes 363271 | solution.py:68
  (224 shorter events, 172.3 us)
Async XLA Ops:
  7.2 208.6 %copy-start = (bf16[6,384,384]{2,1,0:T(8,128)(2,1)S(1)}, bf16[6,384,384]{2,1,0:T(8,128)(2,1)}, u32[]{:S(2)}) copy-start(bf16[6,384,384]{2,1,0:T(8,128)(2,1)} %param.29) | copy-start | bytes 5308420
  7.2 3.2 copy-start.13
  7.2 195.9 %all-reduce.3.cloned.1.call-start = ((), (), s32[]{:S(2)}) async-start(), calls=%async_computation | async-start | bytes 1179648 | tf_op jit(solution)/shard_map/psum | solution.py:169
  156.1 5.0 %copy-start.2 = (bf16[16,128,128]{2,1,0:T(8,128)(2,1)}, bf16[16,128,128]{2,1,0:T(8,128)(2,1)S(1)}, u32[]{:S(2)}) copy-start(bf16[16,128,128]{2,1,0:T(8,128)(2,1)S(1)} %get-tuple-element.533) | copy-start | bytes 1572868
  203.1 4.9 %collective-permute-start = (f32[3,128,384]{2,1,0:T(8,128)}, f32[3,128,384]{2,1,0:T(8,128)}, u32[]{:S(2)}, u32[]{:S(2)}) collective-permute-start(f32[3,128,384]{2,1,0:T(8,128)} %all-reduce.3.cloned.1.call-done), channel_id=1, source_target_pairs={{0,4},{4,0},{8,12},{12,8},{16,20},{20,16},{24,28},{28,24},{1,5},{5... | collective-permute-start | bytes 1769480 | tf_op jit(solution)/shard_map/ppermute | solution.py:14
  205.8 2.2 copy-start.8
  205.8 4.1 copy-start.5
  209.9 0.7 copy-start.6
  216.7 16.2 %copy-start.3 = (bf16[384,384]{1,0:T(8,128)(2,1)S(1)}, bf16[384,384]{1,0:T(8,128)(2,1)}, u32[]{:S(2)}) copy-start(bf16[384,384]{1,0:T(8,128)(2,1)} %get-tuple-element.300) | copy-start | bytes 884740
  216.7 11.8 %collective-permute-start.1 = (f32[2,128,384]{2,1,0:T(8,128)}, f32[2,128,384]{2,1,0:T(8,128)}, u32[]{:S(2)}, u32[]{:S(2)}) collective-permute-start(f32[2,128,384]{2,1,0:T(8,128)} %fusion.68), channel_id=1, source_target_pairs={{0,8},{4,12},{8,0},{12,4},{16,24},{20,28},{24,16},{28,20},{1,9},{5... | collective-permute-start | bytes 1179656 | tf_op jit(solution)/shard_map/ppermute | solution.py:14
  230.7 0.7 copy-start.7
  238.2 8.9 %copy-start.4 = (bf16[384,384]{1,0:T(8,128)(2,1)S(1)}, bf16[384,384]{1,0:T(8,128)(2,1)}, u32[]{:S(2)}) copy-start(bf16[384,384]{1,0:T(8,128)(2,1)} %get-tuple-element.298) | copy-start | bytes 884740
  238.2 6.8 %collective-permute-start.2 = (f32[1,128,384]{2,1,0:T(8,128)}, f32[1,128,384]{2,1,0:T(8,128)}, u32[]{:S(2)}, u32[]{:S(2)}) collective-permute-start(f32[1,128,384]{2,1,0:T(8,128)} %slice_add_fusion), channel_id=1, source_target_pairs={{0,16},{4,20},{8,24},{12,28},{16,0},{20,4},{24,8},{28,12},{1,17},{... | collective-permute-start | bytes 589832 | tf_op jit(solution)/shard_map/ppermute | solution.py:14
  242.7 10.9 %copy-start.10 = (f32[128,128]{0,1:T(8,128)S(1)}, f32[128,128]{0,1:T(8,128)}, u32[]{:S(2)}) copy-start(f32[128,128]{0,1:T(8,128)} %get-tuple-element.311) | copy-start | bytes 196612
  242.7 10.9 %copy-start.11 = (f32[128,128]{0,1:T(8,128)S(1)}, f32[128,128]{0,1:T(8,128)}, u32[]{:S(2)}) copy-start(f32[128,128]{0,1:T(8,128)} %get-tuple-element.315) | copy-start | bytes 196612
  242.7 10.9 %copy-start.12 = (f32[128,128]{0,1:T(8,128)S(1)}, f32[128,128]{0,1:T(8,128)}, u32[]{:S(2)}) copy-start(f32[128,128]{0,1:T(8,128)} %get-tuple-element.313) | copy-start | bytes 196612
  257.9 5.6 %copy-start.9 = (f32[128,128]{0,1:T(8,128)S(1)}, f32[128,128]{0,1:T(8,128)}, u32[]{:S(2)}) copy-start(f32[128,128]{0,1:T(8,128)} %get-tuple-element.329) | copy-start | bytes 196612
  257.9 6.5 %copy-start.1 = (f32[2048,128]{0,1:T(8,128)S(1)}, f32[2048,128]{0,1:T(8,128)}, u32[]{:S(2)}) copy-start(f32[2048,128]{0,1:T(8,128)} %copy.24) | copy-start | bytes 3145732
Sparse Core Ops, SparseCore 0:
  161.3 41.8 all-reduce.2
where the time goes:
time: 417 us; the launch traced here: 410 us
  loops' own time  124 us (30%)
  matrix products  118 us (28%)
  local copies, waits for them, and re-layouts  55.8 us (13%)
  waiting for transfers between devices  52.9 us (13%)
  other arithmetic  42.3 us (10%)
  between operations  14.3 us (3%)
    another operation x1, loops' own time, local_forward(): lax.scan(advance, start, (blocks, inverse, padded, targets, orders))  62.2 us
    another operation x1, loops' own time, local_backward(): lax.scan(retreat, start, (remains, inverse, padded, targets, orders), rev...  61.4 us
    dot_general x32, matrix products, apply_lower(): jnp.dot(matrix, vector.astype(jnp.bfloat16), preferred_element_type=jnp.f...  52.3 us
    psum x1, waiting for transfers between devices, on_device(): updates = lax.psum(partials, 'rep')  42 us
    dynamic_slice x64, local copies, waits for them, and re-layouts, local_forward(): lax.scan(advance, start, (blocks, inverse, padded, targets, orders))  38.9 us
    dot_general x16, matrix products, apply_upper(): jnp.dot(matrix.T, vector.astype(jnp.bfloat16), preferred_element_type=jnp...  27.7 us
    another operation x32, other arithmetic  24.8 us
    dot_general x11, matrix products, right_upper(): jnp.dot(vector_rows.astype(jnp.bfloat16), matrix, preferred_element_type=...  14 us
  transfers between devices with their start and end apart: 4, of which 3 were waited for; matrix products, arithmetic and copies ran while one was open for 2% of the time, Pallas kernels for 0%

commit v1 on v0

v1 whole, which is shorter than its diff:
```python
import functools

import jax
import jax.numpy as jnp
from jax import lax
from jax.experimental import pallas as pl
from jax.experimental.pallas import tpu as pltpu
from jax.sharding import PartitionSpec as P

F32 = jnp.float32
BF16 = jnp.bfloat16
MESH = pl.DeviceIdType.MESH


def nn(a, b):
    return jnp.dot(a, b, preferred_element_type=F32)


def nt(a, b):
    return lax.dot_general(a, b, (((1,), (1,)), ((), ())), preferred_element_type=F32)


def body(
    nleaf,
    nrep,
    par,
    right_hbm,
    inv_hbm,
    below_hbm,
    coup_hbm,
    sright_hbm,
    sinv_hbm,
    slow_hbm,
    pcoup_hbm,
    out_hbm,
    sep_hbm,
    right,
    inv,
    below,
    coup,
    sright,
    sinv,
    slow,
    pcoup,
    ctr,
    mfw,
    wbw,
    pj,
    x,
    eb,
    s0,
    tmat,
    qmat,
    umat,
    srt,
    part,
    pc,
    ph,
    zr,
    rem,
    lr,
    sol,
    out_v,
    sep_v,
    in_sem,
    core_s,
    core_r,
    z_s,
    z_r,
    l_s,
    l_r,
    g_s,
    g_r,
    gc_s,
    gc_r,
    out_sem,
):
    lev = coup.shape[0]
    lb = inv.shape[0]
    nb = inv.shape[1]
    s = coup.shape[1]
    sb = s // nb
    leaf = lax.axis_index("leaf")
    rep = lax.axis_index("rep")
    core = lax.rem(leaf, 2)
    mate = leaf + 1 - 2 * core

    def other_rep(d):
        return lax.rem(rep + d, nrep)

    def other_leaf(height):
        step = 1 << (height - 1)
        bit = lax.rem(leaf // step, 2)
        return leaf + step - 2 * step * bit

    numbers = [(nleaf >> h) - 1 + leaf // (1 << h) for h in range(1, lev + 1)]

    loads = [
        pltpu.make_async_copy(inv_hbm, inv, in_sem.at[0]),
        pltpu.make_async_copy(right_hbm, right, in_sem.at[1]),
        pltpu.make_async_copy(below_hbm, below, in_sem.at[2]),
        pltpu.make_async_copy(coup_hbm, coup, in_sem.at[3]),
    ]
    sep_loads = []
    for h in range(lev):
        n = numbers[h]
        base = 4 + 4 * h
        sep_loads.append(pltpu.make_async_copy(sinv_hbm.at[n], sinv.at[h], in_sem.at[base]))
        sep_loads.append(pltpu.make_async_copy(slow_hbm.at[n], slow.at[h], in_sem.at[base + 1]))
        sep_loads.append(pltpu.make_async_copy(sright_hbm.at[n], sright.at[h], in_sem.at[base + 2]))
        if h < lev - 1:
            sep_loads.append(
                pltpu.make_async_copy(pcoup_hbm.at[n - 1], pcoup.at[h], in_sem.at[base + 3])
            )
    for c in loads + sep_loads:
        c.start()

    barrier = pltpu.get_barrier_semaphore()
    peers = [(mate, rep)]
    peers += [(leaf, other_rep(d)) for d in range(1, nrep)]
    peers += [(other_leaf(h), rep) for h in range(2, lev + 1)]
    for peer in peers:
        pl.semaphore_signal(barrier, inc=1, device_id=peer, device_id_type=MESH)

    loads[0].wait()
    loads[1].wait()
    for k in range(lb):
        ctr[k] = nt(right[k].T.astype(BF16), inv[k])
    loads[2].wait()
    for k in range(lb - 1):
        mfw[k] = nn(inv[par[k]], below[k]).astype(BF16)
    for k in range(lb):
        acc = ctr[k]
        for j in range(k):
            acc = acc - jnp.where(par[j] == k, 1.0, 0.0) * pj[j]
        fb = acc.astype(BF16)
        x[k] = fb
        if k < lb - 1:
            pj[k] = nt(fb, mfw[k])

    pl.semaphore_wait(barrier, len(peers))
    loads[3].wait()
    fwd = jnp.concatenate([x[k] for k in range(lb)], axis=1)
    half = part.shape[2]
    core_copies = []
    for h in range(lev):
        prod = nt(fwd, coup[h])
        part[h, 0] = prod[:half]
        part[h, 1] = prod[half:]
        c = pltpu.make_async_remote_copy(
            src_ref=part.at[h, 1 - core],
            dst_ref=pc.at[h],
            send_sem=core_s.at[h],
            recv_sem=core_r.at[h],
            device_id=(mate, rep),
            device_id_type=MESH,
        )
        c.start()
        core_copies.append(c)

    for c in sep_loads:
        c.wait()

    def prepare(h):
        def low(i, j):
            return slow[h, i * nb : (i + 1) * nb, j * nb : (j + 1) * nb]

        t = {}
        for j in range(sb):
            t[j, j] = sinv[h, j]
            for i in range(j + 1, sb):
                total = nn(low(i, j), t[j, j])
                for m in range(j + 1, i):
                    total = total + nn(low(i, m), t[m, j])
                t[i, j] = (-nn(sinv[h, i], total.astype(BF16))).astype(BF16)
        for i in range(sb):
            for j in range(sb):
                block = t[i, j] if i >= j else jnp.zeros((nb, nb), BF16)
                tmat[h, i * nb : (i + 1) * nb, j * nb : (j + 1) * nb] = block
        full = tmat[h]
        umat[h] = lax.dot_general(
            full, full, (((0,), (0,)), ((), ())), preferred_element_type=F32
        ).astype(BF16)
        if h < lev - 1:
            qmat[h] = nn(pcoup[h], full).astype(BF16)
        srt[h] = sright[h].T.reshape(srt.shape[1:])

    prepare(0)

    rep_copies = []
    for h in range(lev):
        core_copies[h].wait()
        ph[h] = part[h, core].reshape(ph.shape[1:]) + pc[h].reshape(ph.shape[1:])
        row = []
        for d in range(1, nrep):
            c = pltpu.make_async_remote_copy(
                src_ref=ph.at[h, other_rep(d)],
                dst_ref=zr.at[h, d - 1],
                send_sem=z_s.at[h, d - 1],
                recv_sem=z_r.at[h, d - 1],
                device_id=(leaf, other_rep(d)),
                device_id_type=MESH,
            )
            c.start()
            row.append(c)
        rep_copies.append(row)

    for h in range(1, lev):
        prepare(h)

    for k in range(lb - 1):
        wbw[k, :nb] = inv[k]
        wbw[k, nb:] = (-nn(below[k], inv[k])).astype(BF16)

    def back_step(k):
        lanes = slice(k * nb, (k + 1) * nb)
        for g in range(lev + 1):
            if g == 0:
                rows = slice(0, x.shape[1])
                mine = x[k]
            else:
                rows = slice(x.shape[1] + (g - 1) * s, x.shape[1] + g * s)
                mine = coup[g - 1, :, lanes]
            if k == lb - 1:
                value = nn(mine, inv[k])
            else:
                value = nn(jnp.concatenate([mine, eb[par[k], rows]], axis=1), wbw[k])
            eb[k, rows] = value.astype(BF16)
            if g == 0:
                s0[k] = value

    steps = list(range(lb - 1, -1, -1))
    first = (lb * 5) // 8
    rest = lb - first
    for k in steps[:first]:
        back_step(k)
    steps = steps[first:]
    share = -(-rest // max(lev - 1, 1))

    slot = core * nrep + rep
    leaf_copies = {}

    def send_leaf(height, j):
        c = pltpu.make_async_remote_copy(
            src_ref=rem.at[height - 2, j],
            dst_ref=lr.at[height - 2, j],
            send_sem=l_s.at[height - 2, j],
            recv_sem=l_r.at[height - 2, j],
            device_id=(other_leaf(height), rep),
            device_id_type=MESH,
        )
        c.start()
        leaf_copies[height, j] = c

    def total_of(h):
        total = ph[h, rep]
        for c in rep_copies[h]:
            c.wait()
        for d in range(1, nrep):
            total = total + zr[h, d - 1]
        return total

    residues = []
    for height in range(1, lev + 1):
        h = height - 1
        if height == 1:
            now = total_of(0)
        else:
            leaf_copies[height, h].wait()
            now = rem[height - 2, h] + lr[height - 2, h]
        residue = (srt[h, slot] - now).astype(BF16)
        residues.append(residue)
        if height < lev:
            up = nt(residue, qmat[h])
            for j in range(height, lev):
                if height == 1:
                    value = total_of(j)
                else:
                    leaf_copies[height, j].wait()
                    value = rem[height - 2, j] + lr[height - 2, j]
                if j == height:
                    value = value + up
                rem[height - 1, j] = value
                send_leaf(height + 1, j)
            for k in steps[:share]:
                back_step(k)
            steps = steps[share:]

    gather_copies = []
    above = None
    for h in range(lev - 1, -1, -1):
        value = nn(residues[h], umat[h])
        if above is not None:
            value = value - nn(above, qmat[h])
        above = value.astype(BF16)
        sol[h, slot] = value
        row = []
        for d in range(1, nrep):
            c = pltpu.make_async_remote_copy(
                src_ref=sol.at[h, slot],
                dst_ref=sol.at[h, slot],
                send_sem=g_s.at[h, d - 1],
                recv_sem=g_r.at[h, d - 1],
                device_id=(leaf, other_rep(d)),
                device_id_type=MESH,
            )
            c.start()
            row.append(c)
        gather_copies.append(row)
    mate_copies = []
    for i, h in enumerate(range(lev - 1, -1, -1)):
        for c in gather_copies[i]:
            c.wait()
        c = pltpu.make_async_remote_copy(
            src_ref=sol.at[h, pl.ds(core * nrep, nrep)],
            dst_ref=sol.at[h, pl.ds(core * nrep, nrep)],
            send_sem=gc_s.at[h],
            recv_sem=gc_r.at[h],
            device_id=(mate, rep),
            device_id_type=MESH,
        )
        c.start()
        mate_copies.append(c)
    out_copies = []
    for i, h in enumerate(range(lev - 1, -1, -1)):
        mate_copies[i].wait()
        whole = sol[h].reshape(x.shape[1], s)
        rounded = whole.astype(BF16)
        rows = slice(x.shape[1] + h * s, x.shape[1] + (h + 1) * s)
        for k in range(lb):
            value = s0[k] - nn(rounded, eb[k, rows])
            if h > 0:
                s0[k] = value
            else:
                out_v[k] = value.T
                if k % 4 == 3:
                    part_k = pl.ds(k - 3, 4)
                    c = pltpu.make_async_copy(
                        out_v.at[part_k], out_hbm.at[part_k], out_sem.at[lev + k // 4]
                    )
                    c.start()
                    out_copies.append(c)
        sep_v[h] = whole.T
        c = pltpu.make_async_copy(sep_v.at[h], sep_hbm.at[h], out_sem.at[h])
        c.start()
        out_copies.append(c)
    for c in out_copies:
        c.wait()


def on_device(
    nleaf,
    nrep,
    local_right,
    local_inverse,
    local_below,
    local_parent,
    local_coupling,
    separator_right,
    separator_inverse,
    separator_lower,
    parent_coupling,
):
    _, _, lev, s, rows = local_coupling.shape
    lb, nb = local_inverse.shape[2:4]
    r = local_right.shape[3]
    w = r // (2 * nrep)
    sb = s // nb
    any_spec = pl.BlockSpec(memory_space=pl.ANY)
    scratch = [
        pltpu.VMEM((lb, nb, r), F32),
        pltpu.VMEM((lb, nb, nb), BF16),
        pltpu.VMEM((lb - 1, nb, nb), BF16),
        pltpu.VMEM((lev, s, rows), BF16),
        pltpu.VMEM((lev, s, r), F32),
        pltpu.VMEM((lev, sb, nb, nb), BF16),
        pltpu.VMEM((lev, s, s), BF16),
        pltpu.VMEM((lev, s, s), BF16),
        pltpu.VMEM((lb, r, nb), F32),
        pltpu.VMEM((lb - 1, nb, nb), BF16),
        pltpu.VMEM((lb - 1, 2 * nb, nb), BF16),
        pltpu.VMEM((lb - 1, r, nb), F32),
        pltpu.VMEM((lb, r, nb), BF16),
        pltpu.VMEM((lb, r + lev * s, nb), BF16),
        pltpu.VMEM((lb, r, nb), F32),
        pltpu.VMEM((lev, s, s), BF16),
        pltpu.VMEM((lev, s, s), BF16),
        pltpu.VMEM((lev, s, s), BF16),
        pltpu.VMEM((lev, 2 * nrep, w, s), F32),
        pltpu.VMEM((lev, 2, r // 2, s), F32),
        pltpu.VMEM((lev, r // 2, s), F32),
        pltpu.VMEM((lev, nrep, w, s), F32),
        pltpu.VMEM((lev, nrep - 1, w, s), F32),
        pltpu.VMEM((lev - 1, lev, w, s), F32),
        pltpu.VMEM((lev - 1, lev, w, s), F32),
        pltpu.VMEM((lev, 2 * nrep, w, s), F32),
        pltpu.VMEM((lb, nb, r), F32),
        pltpu.VMEM((lev, s, r), F32),
    ] + [
        pltpu.SemaphoreType.DMA(shape)
        for shape in (
            (4 + 4 * lev,),
            (lev,),
            (lev,),
            (lev, nrep - 1),
            (lev, nrep - 1),
            (lev - 1, lev),
            (lev - 1, lev),
            (lev, nrep - 1),
            (lev, nrep - 1),
            (lev,),
            (lev,),
            (lev + lb // 4,),
        )
    ]
    local, sep = pl.pallas_call(
        functools.partial(body, nleaf, nrep),
        out_shape=(
            jax.ShapeDtypeStruct((lb, nb, r), F32),
            jax.ShapeDtypeStruct((lev, s, r), F32),
        ),
        in_specs=[pl.BlockSpec(memory_space=pltpu.SMEM)] + [any_spec] * 8,
        out_specs=(any_spec, any_spec),
        scratch_shapes=scratch,
        compiler_params=pltpu.CompilerParams(
            collective_id=0, has_side_effects=True, vmem_limit_bytes=48 * 2**20
        ),
        name="wiener_solve",
    )(
        local_parent[0, 0],
        local_right[0, 0].reshape(lb, nb, r),
        local_inverse[0, 0],
        local_below[0, 0],
        local_coupling[0, 0],
        separator_right,
        separator_inverse,
        separator_lower,
        parent_coupling,
    )
    return local.reshape(1, 1, rows, r), sep[None]


def solution(mesh):
    in_specs = (
        P("leaf", "rep", None, None),
        P("leaf", "rep", None, None, None),
        P("leaf", "rep", None, None, None),
        P("leaf", "rep", None),
        P("leaf", "rep", None, None, None),
        P(),
        P(),
        P(),
        P(),
    )
    out_specs = (P("leaf", "rep", None, None), P("leaf", None, None, None))
    return jax.shard_map(
        functools.partial(on_device, mesh.shape["leaf"], mesh.shape["rep"]),
        mesh=mesh,
        in_specs=in_specs,
        out_specs=out_specs,
        check_vma=False,
    )
```

time: 417 us -> 47.8 us (0.11); the launches traced: 410 us -> 47.5 us
  loops' own time: 124 us -> 0 us
  matrix products: 118 us -> 0 us
  waiting for transfers between devices: 52.9 us -> 0 us
  local copies, waits for them, and re-layouts: 55.8 us -> 8.17 us
  other arithmetic: 42.3 us -> 0 us
  Pallas kernels: 0 us -> 38.7 us
  between operations: 14.3 us -> 0.66 us
    another operation x2 -> x0, loops' own time: 124 us -> none  [the longest x1 62.2 us: local_forward(): lax.scan(advance, start, (blocks, inverse, padded, targets, orders))]
    dot_general x72 -> x0, matrix products: 118 us -> none  [the longest x32 52.3 us: apply_lower(): jnp.dot(matrix, vector.astype(jnp.bfloat16), preferred_element_type=jnp.f...]
    dynamic_slice x68 -> x0, local copies, waits for them, and re-layouts: 45.1 us -> none  [the longest x64 38.9 us: local_forward(): lax.scan(advance, start, (blocks, inverse, padded, targets, orders))]
    psum x1 -> x0, waiting for transfers between devices: 42 us -> none  [on_device(): updates = lax.psum(partials, 'rep')]
    pallas_call x0 -> x1, Pallas kernels: none -> 38.7 us  [on_device(): pl.pallas_call(functools.partial(body, nleaf, nrep), out_shape=(jax.Shape...]
    another operation x34 -> x0, other arithmetic: 25.8 us -> none
    ppermute x3 -> x0, waiting for transfers between devices: 11 us -> none  [swapped(): return lax.ppermute(value, axis, pairs)]
    scatter x16 -> x0, other arithmetic: 10.5 us -> none  [retreat(): carried = carried.at[number].set(result.astype(jnp.bfloat16))]
  transfers between devices with their start and end apart: 4 -> 0, of which waited for: 3 -> 0; matrix products, arithmetic and copies ran while one was open for 2% -> 0% of each run, Pallas kernels for 0% -> 0%
where the time goes in v1:
time: 47.8 us; the launch traced here: 47.5 us
  Pallas kernels  38.7 us (81%)
  local copies, waits for them, and re-layouts  8.17 us (17%)
  between operations  0.66 us (1%)
    pallas_call x1, Pallas kernels, on_device(): pl.pallas_call(functools.partial(body, nleaf, nrep), out_shape=(jax.Shape...  38.7 us
    unnamed x14, local copies, waits for them, and re-layouts  8.17 us

profile of v1, /device:TPU:0, one launch (start us, length us, event | category | flops | bytes accessed | tf_op | source)
XLA Modules:
  0.0 47.5 jit_solution(12892591552102291120)
XLA Ops:
  0.6 0.0 copy-start
  0.6 1.3 %copy-done = f32[7,384,128]{2,1,0:T(8,128)S(1)} copy-done((f32[7,384,128]{2,1,0:T(8,128)S(1)}, f32[7,384,128]{2,1,0:T(8,128)}, u32[]{:S(2)}) %copy-start) | copy-done | bytes 1376280
  2.0 0.0 copy-start.1
  2.0 1.2 %copy-done.1 = f32[1,1,2048,128]{3,2,1,0:T(8,128)S(1)} copy-done((f32[1,1,2048,128]{3,2,1,0:T(8,128)S(1)}, f32[1,1,2048,128]{3,2,1,0:T(8,128)}, u32[]{:S(2)}) %copy-start.1) | copy-done | bytes 1048600
  3.2 0.0 copy-start.2
  3.2 1.1 %copy-done.2 = bf16[7,3,128,128]{3,2,1,0:T(8,128)(2,1)S(1)} copy-done((bf16[7,3,128,128]{3,2,1,0:T(8,128)(2,1)S(1)}, bf16[7,3,128,128]{3,2,1,0:T(8,128)(2,1)}, u32[]{:S(2)}) %copy-start.2) | copy-done | bytes 688152
  4.3 0.0 copy-start.3
  4.3 1.0 %copy-done.3 = bf16[1,1,16,128,128]{4,3,2,1,0:T(8,128)(2,1)S(1)} copy-done((bf16[1,1,16,128,128]{4,3,2,1,0:T(8,128)(2,1)S(1)}, bf16[1,1,16,128,128]{4,3,2,1,0:T(8,128)(2,1)}, u32[]{:S(2)}) %copy-start.3) | copy-done | bytes 524312
  5.3 0.0 copy-start.4
  5.3 1.0 %copy-done.4 = bf16[1,1,15,128,128]{4,3,2,1,0:T(8,128)(2,1)S(1)} copy-done((bf16[1,1,15,128,128]{4,3,2,1,0:T(8,128)(2,1)S(1)}, bf16[1,1,15,128,128]{4,3,2,1,0:T(8,128)(2,1)}, u32[]{:S(2)}) %copy-start.4) | copy-done | bytes 491544
  6.4 0.0 copy-start.5
  6.4 0.7 %copy-done.5 = s32[1,1,15]{2,1,0:T(1,128)S(1)} copy-done((s32[1,1,15]{2,1,0:T(1,128)S(1)}, s32[1,1,15]{2,1,0:T(1,128)}, u32[]{:S(2)}) %copy-start.5) | copy-done | bytes 84
  7.0 38.7 %wiener_solve.1 = (f32[16,128,128]{2,1,0:T(8,128)S(1)}, f32[3,384,128]{2,1,0:T(8,128)S(1)}) custom-call(s32[15]{0:T(128)S(1)} %bitcast.12, f32[16,128,128]{2,1,0:T(8,128)S(1)} %bitcast.7, bf16[16,128,128]{2,1,0:T(8,128)(2,1)S(1)} %bitcast.10, bf16[15,128,128]{2,1,0:T(8,128)(2,1)S(1)} %bitcast.11, bf16[3,384,2048]{2,1,0:T(8,128)(2,1)} %bitcast.13, ...), custom_call_target="tpu_custom_call" | custom-call | tf_op jit(solution)/shard_map/wiener_solve/pallas_call | solution.py:416
  45.7 1.0 %copy.13 = f32[1,1,2048,128]{3,2,1,0:T(8,128)} copy(f32[1,1,2048,128]{3,2,1,0:T(8,128)S(1)} %bitcast.8) | data formatting | bytes 2097152
  46.7 0.8 %copy.14 = f32[1,3,384,128]{3,2,1,0:T(8,128)} copy(f32[1,3,384,128]{3,2,1,0:T(8,128)S(1)} %bitcast.9) | data formatting | bytes 1179648
Async XLA Ops:
  0.6 1.3 %copy-start = (f32[7,384,128]{2,1,0:T(8,128)S(1)}, f32[7,384,128]{2,1,0:T(8,128)}, u32[]{:S(2)}) copy-start(f32[7,384,128]{2,1,0:T(8,128)} %sright_hbm.1) | copy-start | bytes 4128772
  2.0 1.2 %copy-start.1 = (f32[1,1,2048,128]{3,2,1,0:T(8,128)S(1)}, f32[1,1,2048,128]{3,2,1,0:T(8,128)}, u32[]{:S(2)}) copy-start(f32[1,1,2048,128]{3,2,1,0:T(8,128)} %param.9) | copy-start | bytes 3145732
  3.2 1.1 %copy-start.2 = (bf16[7,3,128,128]{3,2,1,0:T(8,128)(2,1)S(1)}, bf16[7,3,128,128]{3,2,1,0:T(8,128)(2,1)}, u32[]{:S(2)}) copy-start(bf16[7,3,128,128]{3,2,1,0:T(8,128)(2,1)} %sinv_hbm.1) | copy-start | bytes 2064388
  4.3 1.0 %copy-start.3 = (bf16[1,1,16,128,128]{4,3,2,1,0:T(8,128)(2,1)S(1)}, bf16[1,1,16,128,128]{4,3,2,1,0:T(8,128)(2,1)}, u32[]{:S(2)}) copy-start(bf16[1,1,16,128,128]{4,3,2,1,0:T(8,128)(2,1)} %param.10) | copy-start | bytes 1572868
  5.3 1.0 %copy-start.4 = (bf16[1,1,15,128,128]{4,3,2,1,0:T(8,128)(2,1)S(1)}, bf16[1,1,15,128,128]{4,3,2,1,0:T(8,128)(2,1)}, u32[]{:S(2)}) copy-start(bf16[1,1,15,128,128]{4,3,2,1,0:T(8,128)(2,1)} %param.11) | copy-start | bytes 1474564
  6.4 0.7 %copy-start.5 = (s32[1,1,15]{2,1,0:T(1,128)S(1)}, s32[1,1,15]{2,1,0:T(1,128)}, u32[]{:S(2)}) copy-start(s32[1,1,15]{2,1,0:T(1,128)} %param.12) | copy-start | bytes 184

commit v2 on v1

--- a/solution.py
+++ b/solution.py
@@ -23,7 +23,7 @@
 def body(
     nleaf,
     nrep,
-    par,
+    par_hbm,
     right_hbm,
     inv_hbm,
     below_hbm,
@@ -34,6 +34,7 @@
     pcoup_hbm,
     out_hbm,
     sep_hbm,
+    par,
     right,
     inv,
     below,
@@ -42,6 +43,7 @@
     sinv,
     slow,
     pcoup,
+    invc,
     ctr,
     mfw,
     wbw,
@@ -100,11 +102,12 @@
         pltpu.make_async_copy(right_hbm, right, in_sem.at[1]),
         pltpu.make_async_copy(below_hbm, below, in_sem.at[2]),
         pltpu.make_async_copy(coup_hbm, coup, in_sem.at[3]),
+        pltpu.make_async_copy(par_hbm, par, in_sem.at[4]),
     ]
     sep_loads = []
     for h in range(lev):
         n = numbers[h]
-        base = 4 + 4 * h
+        base = 5 + 4 * h
         sep_loads.append(pltpu.make_async_copy(sinv_hbm.at[n], sinv.at[h], in_sem.at[base]))
         sep_loads.append(pltpu.make_async_copy(slow_hbm.at[n], slow.at[h], in_sem.at[base + 1]))
         sep_loads.append(pltpu.make_async_copy(sright_hbm.at[n], sright.at[h], in_sem.at[base + 2]))
@@ -122,25 +125,49 @@
     for peer in peers:
         pl.semaphore_signal(barrier, inc=1, device_id=peer, device_id_type=MESH)
 
+    npair = lb // 2
+    wide = 2 * nb
     loads[0].wait()
+    loads[2].wait()
+    loads[4].wait()
+    for q in range(npair):
+        lo, hi = 2 * q, 2 * q + 1
+        inside = jnp.where(par[lo] == hi, 1.0, 0.0)
+        scaled = nn(below[lo], inv[lo])
+        corner = (-inside * nn(inv[hi], scaled.astype(BF16))).astype(BF16)
+        zero = jnp.zeros((nb, nb), BF16)
+        wbw[q, :nb, :nb] = inv[lo]
+        wbw[q, :nb, nb:] = zero
+        wbw[q, nb:wide, :nb] = corner
+        wbw[q, nb:wide, nb:] = inv[hi]
+        invc[lo, :nb] = inv[lo]
+        invc[lo, nb:] = corner
+        invc[hi, :nb] = zero
+        invc[hi, nb:] = inv[hi]
+        if q < npair - 1:
+            wbw[q, wide : wide + nb, :nb] = ((inside - 1.0) * scaled).astype(BF16)
+            wbw[q, wide : wide + nb, nb:] = zero
+
+    for b in range(lb - 2):
+        mfw[b] = nn(invc[par[b]], below[b]).astype(BF16)
     loads[1].wait()
-    for k in range(lb):
-        ctr[k] = nt(right[k].T.astype(BF16), inv[k])
-    loads[2].wait()
-    for k in range(lb - 1):
-        mfw[k] = nn(inv[par[k]], below[k]).astype(BF16)
-    for k in range(lb):
-        acc = ctr[k]
-        for j in range(k):
-            acc = acc - jnp.where(par[j] == k, 1.0, 0.0) * pj[j]
+    for q in range(npair):
+        rows = jnp.concatenate([right[2 * q].T, right[2 * q + 1].T], axis=1)
+        ctr[q] = nt(rows.astype(BF16), wbw[q, :wide])
+    for q in range(npair):
+        acc = ctr[q]
+        for b in range(2 * q):
+            hit = (par[b] >= 2 * q) & (par[b] <= 2 * q + 1)
+            acc = acc - jnp.where(hit, 1.0, 0.0) * pj[b]
         fb = acc.astype(BF16)
-        x[k] = fb
-        if k < lb - 1:
-            pj[k] = nt(fb, mfw[k])
+        x[q] = fb
+        if q < npair - 1:
+            pj[2 * q] = nt(fb[:, :nb], mfw[2 * q])
+            pj[2 * q + 1] = nt(fb[:, nb:], mfw[2 * q + 1])
 
     pl.semaphore_wait(barrier, len(peers))
     loads[3].wait()
-    fwd = jnp.concatenate([x[k] for k in range(lb)], axis=1)
+    fwd = jnp.concatenate([x[q] for q in range(npair)], axis=1)
     half = part.shape[2]
     core_copies = []
     for h in range(lev):
@@ -208,32 +235,36 @@
     for h in range(1, lev):
         prepare(h)
 
-    for k in range(lb - 1):
-        wbw[k, :nb] = inv[k]
-        wbw[k, nb:] = (-nn(below[k], inv[k])).astype(BF16)
-
-    def back_step(k):
-        lanes = slice(k * nb, (k + 1) * nb)
+    for q in range(npair - 1):
+        wbw[q, wide + nb :] = (-nn(below[2 * q + 1], wbw[q, nb:wide])).astype(BF16)
+
+    r = x.shape[1]
+
+    def back_step(q):
+        lanes = slice(q * wide, (q + 1) * wide)
         for g in range(lev + 1):
             if g == 0:
-                rows = slice(0, x.shape[1])
-                mine = x[k]
+                rows = slice(0, r)
+                mine = x[q]
             else:
-                rows = slice(x.shape[1] + (g - 1) * s, x.shape[1] + g * s)
+                rows = slice(r + (g - 1) * s, r + g * s)
                 mine = coup[g - 1, :, lanes]
-            if k == lb - 1:
-                value = nn(mine, inv[k])
+            if q == npair - 1:
+                value = nn(mine, wbw[q, :wide])
             else:
-                value = nn(jnp.concatenate([mine, eb[par[k], rows]], axis=1), wbw[k])
-            eb[k, rows] = value.astype(BF16)
+                one = eb[jnp.maximum(par[2 * q], 2 * q + 2), rows]
+                two = eb[par[2 * q + 1], rows]
+                value = nn(jnp.concatenate([mine, one, two], axis=1), wbw[q])
+            eb[2 * q, rows] = value[:, :nb].astype(BF16)
+            eb[2 * q + 1, rows] = value[:, nb:].astype(BF16)
             if g == 0:
-                s0[k] = value
-
-    steps = list(range(lb - 1, -1, -1))
-    first = (lb * 5) // 8
-    rest = lb - first
-    for k in steps[:first]:
-        back_step(k)
+                s0[q] = value
+
+    steps = list(range(npair - 1, -1, -1))
+    first = (npair * 5) // 8
+    rest = npair - first
+    for q in steps[:first]:
+        back_step(q)
     steps = steps[first:]
     share = -(-rest // max(lev - 1, 1))
 
@@ -282,8 +313,8 @@
                     value = value + up
                 rem[height - 1, j] = value
                 send_leaf(height + 1, j)
-            for k in steps[:share]:
-                back_step(k)
+            for q in steps[:share]:
+                back_step(q)
             steps = steps[share:]
 
     gather_copies = []
@@ -307,9 +338,11 @@
             c.start()
             row.append(c)
         gather_copies.append(row)
-    mate_copies = []
-    for i, h in enumerate(range(lev - 1, -1, -1)):
-        for c in gather_copies[i]:
+    mate_copies = {}
+    out_copies = []
+
+    def share_with_mate(h):
+        for c in gather_copies[lev - 1 - h]:
             c.wait()
         c = pltpu.make_async_remote_copy(
             src_ref=sol.at[h, pl.ds(core * nrep, nrep)],
@@ -320,32 +353,57 @@
             device_id_type=MESH,
         )
         c.start()
-        mate_copies.append(c)
-    out_copies = []
-    for i, h in enumerate(range(lev - 1, -1, -1)):
-        mate_copies[i].wait()
-        whole = sol[h].reshape(x.shape[1], s)
-        rounded = whole.astype(BF16)
-        rows = slice(x.shape[1] + h * s, x.shape[1] + (h + 1) * s)
-        for k in range(lb):
-            value = s0[k] - nn(rounded, eb[k, rows])
-            if h > 0:
-                s0[k] = value
-            else:
-                out_v[k] = value.T
-                if k % 4 == 3:
-                    part_k = pl.ds(k - 3, 4)
-                    c = pltpu.make_async_copy(
-                        out_v.at[part_k], out_hbm.at[part_k], out_sem.at[lev + k // 4]
-                    )
-                    c.start()
-                    out_copies.append(c)
+        mate_copies[h] = c
+
+    def whole_solution(h):
+        mate_copies[h].wait()
+        return sol[h].reshape(r, s)
+
+    def write_separator(h, whole):
         sep_v[h] = whole.T
         c = pltpu.make_async_copy(sep_v.at[h], sep_hbm.at[h], out_sem.at[h])
         c.start()
         out_copies.append(c)
+
+    def weights(q, rows):
+        return jnp.concatenate([eb[2 * q, rows], eb[2 * q + 1, rows]], axis=1)
+
+    for h in range(lev - 1, 0, -1):
+        share_with_mate(h)
+    uppers = [whole_solution(h) for h in range(1, lev)]
+    upper = jnp.concatenate([u.astype(BF16) for u in uppers], axis=1)
+    rows = slice(r + s, r + lev * s)
+    for q in range(npair):
+        s0[q] = s0[q] - nn(upper, weights(q, rows))
+    share_with_mate(0)
+    for h in range(1, lev):
+        write_separator(h, uppers[h - 1])
+    lowest = whole_solution(0)
+    lower = lowest.astype(BF16)
+    rows = slice(r, r + s)
+    for q in range(npair):
+        value = s0[q] - nn(lower, weights(q, rows))
+        out_v[2 * q] = value[:, :nb].T
+        out_v[2 * q + 1] = value[:, nb:].T
+        if q % 2 == 1:
+            part_q = pl.ds(2 * q - 2, 4)
+            c = pltpu.make_async_copy(
+                out_v.at[part_q], out_hbm.at[part_q], out_sem.at[lev + q // 2]
+            )
+            c.start()
+            out_copies.append(c)
+    write_separator(0, lowest)
     for c in out_copies:
         c.wait()
+
+
+def hand_out(local_in, sep_in, local_out, sep_out, sem):
+    first = pltpu.make_async_copy(local_in, local_out, sem.at[0])
+    second = pltpu.make_async_copy(sep_in, sep_out, sem.at[1])
+    first.start()
+    second.start()
+    first.wait()
+    second.wait()
 
 
 def on_device(
@@ -367,7 +425,9 @@
     w = r // (2 * nrep)
     sb = s // nb
     any_spec = pl.BlockSpec(memory_space=pl.ANY)
+    hbm_spec = pl.BlockSpec(memory_space=pltpu.HBM)
     scratch = [
+        pltpu.SMEM((lb - 1,), jnp.int32),
         pltpu.VMEM((lb, nb, r), F32),
         pltpu.VMEM((lb, nb, nb), BF16),
         pltpu.VMEM((lb - 1, nb, nb), BF16),
@@ -376,13 +436,14 @@
         pltpu.VMEM((lev, sb, nb, nb), BF16),
         pltpu.VMEM((lev, s, s), BF16),
         pltpu.VMEM((lev, s, s), BF16),
-        pltpu.VMEM((lb, r, nb), F32),
-        pltpu.VMEM((lb - 1, nb, nb), BF16),
-        pltpu.VMEM((lb - 1, 2 * nb, nb), BF16),
-        pltpu.VMEM((lb - 1, r, nb), F32),
-        pltpu.VMEM((lb, r, nb), BF16),
+        pltpu.VMEM((lb, 2 * nb, nb), BF16),
+        pltpu.VMEM((lb // 2, r, 2 * nb), F32),
+        pltpu.VMEM((lb - 2, 2 * nb, nb), BF16),
+        pltpu.VMEM((lb // 2, 4 * nb, 2 * nb), BF16),
+        pltpu.VMEM((lb - 2, r, 2 * nb), F32),
+        pltpu.VMEM((lb // 2, r, 2 * nb), BF16),
         pltpu.VMEM((lb, r + lev * s, nb), BF16),
-        pltpu.VMEM((lb, r, nb), F32),
+        pltpu.VMEM((lb // 2, r, 2 * nb), F32),
         pltpu.VMEM((lev, s, s), BF16),
         pltpu.VMEM((lev, s, s), BF16),
         pltpu.VMEM((lev, s, s), BF16),
@@ -399,7 +460,7 @@
     ] + [
         pltpu.SemaphoreType.DMA(shape)
         for shape in (
-            (4 + 4 * lev,),
+            (5 + 4 * lev,),
             (lev,),
             (lev,),
             (lev, nrep - 1),
@@ -419,11 +480,11 @@
             jax.ShapeDtypeStruct((lb, nb, r), F32),
             jax.ShapeDtypeStruct((lev, s, r), F32),
         ),
-        in_specs=[pl.BlockSpec(memory_space=pltpu.SMEM)] + [any_spec] * 8,
+        in_specs=[hbm_spec] * 9,
         out_specs=(any_spec, any_spec),
         scratch_shapes=scratch,
         compiler_params=pltpu.CompilerParams(
-            collective_id=0, has_side_effects=True, vmem_limit_bytes=48 * 2**20
+            collective_id=0, has_side_effects=True, vmem_limit_bytes=63 * 2**20
         ),
         name="wiener_solve",
     )(
@@ -437,6 +498,18 @@
         separator_lower,
         parent_coupling,
     )
+    local, sep = pl.pallas_call(
+        hand_out,
+        out_shape=(
+            jax.ShapeDtypeStruct((lb, nb, r), F32),
+            jax.ShapeDtypeStruct((lev, s, r), F32),
+        ),
+        in_specs=[any_spec] * 2,
+        out_specs=(hbm_spec, hbm_spec),
+        scratch_shapes=[pltpu.SemaphoreType.DMA((2,))],
+        compiler_params=pltpu.CompilerParams(vmem_limit_bytes=63 * 2**20),
+        name="hand_out",
+    )(local, sep)
     return local.reshape(1, 1, rows, r), sep[None]
 
 

time: 47.8 us -> 85.4 us (1.79)
  Pallas kernels: 38.7 us -> 84.7 us
  local copies, waits for them, and re-layouts: 8.17 us -> 0 us
    pallas_call x0 -> x1, Pallas kernels: none -> 50.8 us  [on_device(): pl.pallas_call(hand_out, out_shape=(jax.ShapeDtypeStruct((lb, nb, r), F32...]
    unnamed x14 -> x0, local copies, waits for them, and re-layouts: 8.17 us -> none
    pallas_call x1, Pallas kernels: 38.7 us -> 33.9 us  [on_device(): pl.pallas_call(functools.partial(body, nleaf, nrep), out_shape=(jax.Shape...]
where the time goes in v2:
time: 85.4 us; the launch traced here: 85.3 us
  Pallas kernels  84.7 us (99%)
    pallas_call x1, Pallas kernels, on_device(): pl.pallas_call(hand_out, out_shape=(jax.ShapeDtypeStruct((lb, nb, r), F32...  50.8 us
    pallas_call x1, Pallas kernels, on_device(): pl.pallas_call(functools.partial(body, nleaf, nrep), out_shape=(jax.Shape...  33.9 us

profile of v2, /device:TPU:0, one launch (start us, length us, event | category | flops | bytes accessed | tf_op | source)
XLA Modules:
  0.0 85.3 jit_solution(12422249762793596721)
XLA Ops:
  0.6 33.9 %wiener_solve.1 = (f32[16,128,128]{2,1,0:T(8,128)}, f32[3,384,128]{2,1,0:T(8,128)}) custom-call(s32[15]{0:T(128)} %bitcast.11, f32[16,128,128]{2,1,0:T(8,128)} %bitcast.8, bf16[16,128,128]{2,1,0:T(8,128)(2,1)} %bitcast.9, bf16[15,128,128]{2,1,0:T(8,128)(2,1)} %bitcast.10, bf16[3,384,2048]{2,1,0:T(8,128)(2,1)} %bitcast.7, f32[7,384,128]{2,1,0:T(8,128)} %sright_hbm.1, ...), custom_call_target="tpu_custom_call" | custom-call | tf_op jit(solution)/shard_map/wiener_solve/pallas_call | solution.py:477
  34.6 50.8 %hand_out.1 = (f32[16,128,128]{2,1,0:T(8,128)}, f32[3,384,128]{2,1,0:T(8,128)}) custom-call(f32[16,128,128]{2,1,0:T(8,128)} %get-tuple-element.6.local_in, f32[3,384,128]{2,1,0:T(8,128)} %get-tuple-element.7.sep_in), custom_call_target="tpu_custom_call" | custom-call | tf_op jit(solution)/shard_map/hand_out/pallas_call | solution.py:501

commit v3 on v2

--- a/solution.py
+++ b/solution.py
@@ -261,12 +261,13 @@
                 s0[q] = value
 
     steps = list(range(npair - 1, -1, -1))
-    first = (npair * 5) // 8
-    rest = npair - first
-    for q in steps[:first]:
-        back_step(q)
-    steps = steps[first:]
-    share = -(-rest // max(lev - 1, 1))
+
+    def spend(count):
+        for q in steps[:count]:
+            back_step(q)
+        del steps[:count]
+
+    spend(3)
 
     slot = core * nrep + rep
     leaf_copies = {}
@@ -291,40 +292,12 @@
             total = total + zr[h, d - 1]
         return total
 
-    residues = []
-    for height in range(1, lev + 1):
-        h = height - 1
-        if height == 1:
-            now = total_of(0)
-        else:
-            leaf_copies[height, h].wait()
-            now = rem[height - 2, h] + lr[height - 2, h]
-        residue = (srt[h, slot] - now).astype(BF16)
-        residues.append(residue)
-        if height < lev:
-            up = nt(residue, qmat[h])
-            for j in range(height, lev):
-                if height == 1:
-                    value = total_of(j)
-                else:
-                    leaf_copies[height, j].wait()
-                    value = rem[height - 2, j] + lr[height - 2, j]
-                if j == height:
-                    value = value + up
-                rem[height - 1, j] = value
-                send_leaf(height + 1, j)
-            for q in steps[:share]:
-                back_step(q)
-            steps = steps[share:]
-
-    gather_copies = []
-    above = None
-    for h in range(lev - 1, -1, -1):
-        value = nn(residues[h], umat[h])
-        if above is not None:
-            value = value - nn(above, qmat[h])
-        above = value.astype(BF16)
-        sol[h, slot] = value
+    gather_copies = {}
+    mate_copies = {}
+    out_copies = []
+
+    def gather(h, residue):
+        sol[h, slot] = residue
         row = []
         for d in range(1, nrep):
             c = pltpu.make_async_remote_copy(
@@ -337,12 +310,10 @@
             )
             c.start()
             row.append(c)
-        gather_copies.append(row)
-    mate_copies = {}
-    out_copies = []
+        gather_copies[h] = row
 
     def share_with_mate(h):
-        for c in gather_copies[lev - 1 - h]:
+        for c in gather_copies[h]:
             c.wait()
         c = pltpu.make_async_remote_copy(
             src_ref=sol.at[h, pl.ds(core * nrep, nrep)],
@@ -355,34 +326,63 @@
         c.start()
         mate_copies[h] = c
 
-    def whole_solution(h):
+    for height in range(1, lev + 1):
+        h = height - 1
+        if height == 1:
+            now = total_of(0)
+        else:
+            leaf_copies[height, h].wait()
+            now = rem[height - 2, h] + lr[height - 2, h]
+        residue = srt[h, slot] - now
+        gather(h, residue)
+        if height < lev:
+            up = nt(residue.astype(BF16), qmat[h])
+            for j in range(height, lev):
+                if height == 1:
+                    spend(1)
+                    value = total_of(j)
+                else:
+                    leaf_copies[height, j].wait()
+                    value = rem[height - 2, j] + lr[height - 2, j]
+                if j == height:
+                    value = value + up
+                rem[height - 1, j] = value
+                send_leaf(height + 1, j)
+            spend(2)
+            if height > 1:
+                share_with_mate(height - 2)
+    spend(npair)
+    share_with_mate(lev - 2)
+
+    def level_rows(h):
+        return slice(r + h * s, r + (h + 1) * s)
+
+    def weights(q, h):
+        rows = level_rows(h)
+        return jnp.concatenate([eb[2 * q, rows], eb[2 * q + 1, rows]], axis=1)
+
+    def fold(h):
+        for q in range(npair):
+            value = weights(q, h + 1).astype(F32) - nn(qmat[h], weights(q, h))
+            eb[2 * q, level_rows(h + 1)] = value[:, :nb].astype(BF16)
+            eb[2 * q + 1, level_rows(h + 1)] = value[:, nb:].astype(BF16)
+
+    def spread(h):
         mate_copies[h].wait()
-        return sol[h].reshape(r, s)
-
-    def write_separator(h, whole):
-        sep_v[h] = whole.T
-        c = pltpu.make_async_copy(sep_v.at[h], sep_hbm.at[h], out_sem.at[h])
-        c.start()
-        out_copies.append(c)
-
-    def weights(q, rows):
-        return jnp.concatenate([eb[2 * q, rows], eb[2 * q + 1, rows]], axis=1)
-
-    for h in range(lev - 1, 0, -1):
-        share_with_mate(h)
-    uppers = [whole_solution(h) for h in range(1, lev)]
-    upper = jnp.concatenate([u.astype(BF16) for u in uppers], axis=1)
-    rows = slice(r + s, r + lev * s)
+        return nn(sol[h].reshape(r, s).astype(BF16), umat[h])
+
+    spreads = []
+    for h in range(lev - 1):
+        fold(h)
+        spreads.append(spread(h))
+        gb = spreads[h].astype(BF16)
+        for q in range(npair):
+            s0[q] = s0[q] - nn(gb, weights(q, h))
+    share_with_mate(lev - 1)
+    spreads.append(spread(lev - 1))
+    gb = spreads[lev - 1].astype(BF16)
     for q in range(npair):
-        s0[q] = s0[q] - nn(upper, weights(q, rows))
-    share_with_mate(0)
-    for h in range(1, lev):
-        write_separator(h, uppers[h - 1])
-    lowest = whole_solution(0)
-    lower = lowest.astype(BF16)
-    rows = slice(r, r + s)
-    for q in range(npair):
-        value = s0[q] - nn(lower, weights(q, rows))
+        value = s0[q] - nn(gb, weights(q, lev - 1))
         out_v[2 * q] = value[:, :nb].T
         out_v[2 * q + 1] = value[:, nb:].T
         if q % 2 == 1:
@@ -392,18 +392,40 @@
             )
             c.start()
             out_copies.append(c)
-    write_separator(0, lowest)
+    whole = None
+    for h in range(lev - 1, -1, -1):
+        if whole is None:
+            whole = spreads[h]
+        else:
+            whole = spreads[h] - nn(whole.astype(BF16), qmat[h])
+        sep_v[h] = whole.T
+        c = pltpu.make_async_copy(sep_v.at[h], sep_hbm.at[h], out_sem.at[h])
+        c.start()
+        out_copies.append(c)
     for c in out_copies:
         c.wait()
 
 
-def hand_out(local_in, sep_in, local_out, sep_out, sem):
-    first = pltpu.make_async_copy(local_in, local_out, sem.at[0])
-    second = pltpu.make_async_copy(sep_in, sep_out, sem.at[1])
-    first.start()
-    second.start()
-    first.wait()
-    second.wait()
+def hand_out(local_in, sep_in, local_out, sep_out, local_v, sep_v, in_sem, out_sem):
+    loads, stores = [], []
+    chunk = local_v.shape[0] // 4
+    for i in range(4):
+        part = pl.ds(i * chunk, chunk)
+        loads.append(
+            pltpu.make_async_copy(local_in.at[part], local_v.at[part], in_sem.at[i])
+        )
+        stores.append(
+            pltpu.make_async_copy(local_v.at[part], local_out.at[part], out_sem.at[i])
+        )
+    loads.append(pltpu.make_async_copy(sep_in, sep_v, in_sem.at[4]))
+    stores.append(pltpu.make_async_copy(sep_v, sep_out, out_sem.at[4]))
+    for load in loads:
+        load.start()
+    for load, store in zip(loads, stores):
+        load.wait()
+        store.start()
+    for store in stores:
+        store.wait()
 
 
 def on_device(
@@ -506,7 +528,12 @@
         ),
         in_specs=[any_spec] * 2,
         out_specs=(hbm_spec, hbm_spec),
-        scratch_shapes=[pltpu.SemaphoreType.DMA((2,))],
+        scratch_shapes=[
+            pltpu.VMEM((lb, nb, r), F32),
+            pltpu.VMEM((lev, s, r), F32),
+            pltpu.SemaphoreType.DMA((5,)),
+            pltpu.SemaphoreType.DMA((5,)),
+        ],
         compiler_params=pltpu.CompilerParams(vmem_limit_bytes=63 * 2**20),
         name="hand_out",
     )(local, sep)

time: 85.4 us -> 35.8 us (0.42)
  Pallas kernels: 84.7 us -> 35 us
    pallas_call x1, Pallas kernels: 50.8 us -> 2.29 us  [on_device(): pl.pallas_call(hand_out, out_shape=(jax.ShapeDtypeStruct((lb, nb, r), F32...]
    pallas_call x1, Pallas kernels: 33.9 us -> 32.7 us  [on_device(): pl.pallas_call(functools.partial(body, nleaf, nrep), out_shape=(jax.Shape...]
where the time goes in v3:
time: 35.8 us; the launch traced here: 35.6 us
  Pallas kernels  35 us (98%)
  between operations  0.64 us (2%)
    pallas_call x1, Pallas kernels, on_device(): pl.pallas_call(functools.partial(body, nleaf, nrep), out_shape=(jax.Shape...  32.7 us
    pallas_call x1, Pallas kernels, on_device(): pl.pallas_call(hand_out, out_shape=(jax.ShapeDtypeStruct((lb, nb, r), F32...  2.29 us

profile of v3, /device:TPU:0, one launch (start us, length us, event | category | flops | bytes accessed | tf_op | source)
XLA Modules:
  0.0 35.6 jit_solution(8964863243438124484)
XLA Ops:
  0.6 32.7 %wiener_solve.1 = (f32[16,128,128]{2,1,0:T(8,128)}, f32[3,384,128]{2,1,0:T(8,128)}) custom-call(s32[15]{0:T(128)} %bitcast.11, f32[16,128,128]{2,1,0:T(8,128)} %bitcast.8, bf16[16,128,128]{2,1,0:T(8,128)(2,1)} %bitcast.9, bf16[15,128,128]{2,1,0:T(8,128)(2,1)} %bitcast.10, bf16[3,384,2048]{2,1,0:T(8,128)(2,1)} %bitcast.7, f32[7,384,128]{2,1,0:T(8,128)} %sright_hbm.1, ...), custom_call_target="tpu_custom_call" | custom-call | tf_op jit(solution)/shard_map/wiener_solve/pallas_call | solution.py:499
  33.3 2.3 %hand_out.1 = (f32[16,128,128]{2,1,0:T(8,128)}, f32[3,384,128]{2,1,0:T(8,128)}) custom-call(f32[16,128,128]{2,1,0:T(8,128)} %get-tuple-element.6.local_in, f32[3,384,128]{2,1,0:T(8,128)} %get-tuple-element.7.sep_in), custom_call_target="tpu_custom_call" | custom-call | tf_op jit(solution)/shard_map/hand_out/pallas_call | solution.py:523

commit v4 on v3

--- a/solution.py
+++ b/solution.py
@@ -170,7 +170,9 @@
     fwd = jnp.concatenate([x[q] for q in range(npair)], axis=1)
     half = part.shape[2]
     core_copies = []
-    for h in range(lev):
+    rep_copies = []
+
+    def send_core(h):
         prod = nt(fwd, coup[h])
         part[h, 0] = prod[:half]
         part[h, 1] = prod[half:]
@@ -185,37 +187,7 @@
         c.start()
         core_copies.append(c)
 
-    for c in sep_loads:
-        c.wait()
-
-    def prepare(h):
-        def low(i, j):
-            return slow[h, i * nb : (i + 1) * nb, j * nb : (j + 1) * nb]
-
-        t = {}
-        for j in range(sb):
-            t[j, j] = sinv[h, j]
-            for i in range(j + 1, sb):
-                total = nn(low(i, j), t[j, j])
-                for m in range(j + 1, i):
-                    total = total + nn(low(i, m), t[m, j])
-                t[i, j] = (-nn(sinv[h, i], total.astype(BF16))).astype(BF16)
-        for i in range(sb):
-            for j in range(sb):
-                block = t[i, j] if i >= j else jnp.zeros((nb, nb), BF16)
-                tmat[h, i * nb : (i + 1) * nb, j * nb : (j + 1) * nb] = block
-        full = tmat[h]
-        umat[h] = lax.dot_general(
-            full, full, (((0,), (0,)), ((), ())), preferred_element_type=F32
-        ).astype(BF16)
-        if h < lev - 1:
-            qmat[h] = nn(pcoup[h], full).astype(BF16)
-        srt[h] = sright[h].T.reshape(srt.shape[1:])
-
-    prepare(0)
-
-    rep_copies = []
-    for h in range(lev):
+    def send_rep(h):
         core_copies[h].wait()
         ph[h] = part[h, core].reshape(ph.shape[1:]) + pc[h].reshape(ph.shape[1:])
         row = []
@@ -232,8 +204,39 @@
             row.append(c)
         rep_copies.append(row)
 
+    send_core(0)
     for h in range(1, lev):
-        prepare(h)
+        send_core(h)
+        send_rep(h - 1)
+
+    for c in sep_loads:
+        c.wait()
+    levels = range(lev)
+    t = {}
+
+    def low(h, i, j):
+        return slow[h, i * nb : (i + 1) * nb, j * nb : (j + 1) * nb]
+
+    for h in levels:
+        for i in range(sb):
+            t[h, i, i] = sinv[h, i]
+    for gap in range(1, sb):
+        for j in range(sb - gap):
+            i = j + gap
+            totals = [
+                sum(nn(low(h, i, m), t[h, m, j]) for m in range(j, i)) for h in levels
+            ]
+            for h in levels:
+                t[h, i, j] = (-nn(sinv[h, i], totals[h].astype(BF16))).astype(BF16)
+    for h in levels:
+        for i in range(sb):
+            for j in range(sb):
+                block = t[h, i, j] if i >= j else jnp.zeros((nb, nb), BF16)
+                tmat[h, i * nb : (i + 1) * nb, j * nb : (j + 1) * nb] = block
+        if h < lev - 1:
+            qmat[h] = nn(pcoup[h], tmat[h]).astype(BF16)
+        srt[h] = sright[h].T.reshape(srt.shape[1:])
+    send_rep(lev - 1)
 
     for q in range(npair - 1):
         wbw[q, wide + nb :] = (-nn(below[2 * q + 1], wbw[q, nb:wide])).astype(BF16)
@@ -267,7 +270,7 @@
             back_step(q)
         del steps[:count]
 
-    spend(3)
+    spend(2)
 
     slot = core * nrep + rep
     leaf_copies = {}
@@ -353,6 +356,11 @@
                 share_with_mate(height - 2)
     spend(npair)
     share_with_mate(lev - 2)
+    for h in levels:
+        full = tmat[h]
+        umat[h] = lax.dot_general(
+            full, full, (((0,), (0,)), ((), ())), preferred_element_type=F32
+        ).astype(BF16)
 
     def level_rows(h):
         return slice(r + h * s, r + (h + 1) * s)
@@ -374,11 +382,12 @@
     spreads = []
     for h in range(lev - 1):
         fold(h)
+        if h == lev - 2:
+            share_with_mate(lev - 1)
         spreads.append(spread(h))
         gb = spreads[h].astype(BF16)
         for q in range(npair):
             s0[q] = s0[q] - nn(gb, weights(q, h))
-    share_with_mate(lev - 1)
     spreads.append(spread(lev - 1))
     gb = spreads[lev - 1].astype(BF16)
     for q in range(npair):

time: 35.8 us -> 34.6 us (0.966)
  Pallas kernels: 35 us -> 33.9 us
    pallas_call x1, Pallas kernels: 32.7 us -> 31.6 us  [on_device(): pl.pallas_call(functools.partial(body, nleaf, nrep), out_shape=(jax.Shape...]
where the time goes in v4:
time: 34.6 us; the launch traced here: 34.5 us
  Pallas kernels  33.9 us (98%)
  between operations  0.64 us (2%)
    pallas_call x1, Pallas kernels, on_device(): pl.pallas_call(functools.partial(body, nleaf, nrep), out_shape=(jax.Shape...  31.6 us
    pallas_call x1, Pallas kernels, on_device(): pl.pallas_call(hand_out, out_shape=(jax.ShapeDtypeStruct((lb, nb, r), F32...  2.29 us

profile of v4, /device:TPU:0, one launch (start us, length us, event | category | flops | bytes accessed | tf_op | source)
XLA Modules:
  0.0 34.5 jit_solution(13978284244660363001)
XLA Ops:
  0.6 31.6 %wiener_solve.1 = (f32[16,128,128]{2,1,0:T(8,128)}, f32[3,384,128]{2,1,0:T(8,128)}) custom-call(s32[15]{0:T(128)} %bitcast.11, f32[16,128,128]{2,1,0:T(8,128)} %bitcast.8, bf16[16,128,128]{2,1,0:T(8,128)(2,1)} %bitcast.9, bf16[15,128,128]{2,1,0:T(8,128)(2,1)} %bitcast.10, bf16[3,384,2048]{2,1,0:T(8,128)(2,1)} %bitcast.7, f32[7,384,128]{2,1,0:T(8,128)} %sright_hbm.1, ...), custom_call_target="tpu_custom_call" | custom-call | tf_op jit(solution)/shard_map/wiener_solve/pallas_call | solution.py:508
  32.2 2.3 %hand_out.1 = (f32[16,128,128]{2,1,0:T(8,128)}, f32[3,384,128]{2,1,0:T(8,128)}) custom-call(f32[16,128,128]{2,1,0:T(8,128)} %get-tuple-element.6.local_in, f32[3,384,128]{2,1,0:T(8,128)} %get-tuple-element.7.sep_in), custom_call_target="tpu_custom_call" | custom-call | tf_op jit(solution)/shard_map/hand_out/pallas_call | solution.py:532
